TPU v7x, 32 devices: a whole 2x2x4 slice. The times are simulated.
32 devices in a mesh: groups: 2 (over y), blk: 4 (over z), sub: 2 (over x), pair: 2 (over core).
Axes of the slice: x: 2, y: 2, z: 4, core: 2. Of those that a mesh axis runs over, the one named last changes fastest.
Arguments:
- source: bfloat16 [8, 2048, 256], P(('groups', 'blk'), 'sub'), parts along dimension 0, may hold values from -0.5 to 0.5
- target: bfloat16 [64, 512, 256], P(('groups', 'blk'), 'pair'), parts along dimension 0, may hold values from -0.5 to 0.5
- target_slot_index: int32 [64], P('groups'), parts along dimension 0, may hold values from 0 to 31, as said below
- active_block_table: int32 [8, 16], P('groups'), parts along dimension 0, may hold values from -1 to 31, as said below
- active_count: int32 [8], P('groups'), parts along dimension 0, may hold values from 10 to 16, as said below
Outputs:
- row_potential: float32 [8, 2048], P(('groups', 'blk'), 'sub'), parts along dimension 0
- column_potential: float32 [64, 512], P(('groups', 'blk'), 'pair'), parts along dimension 0
There are 2 independent parts, one for each index of `groups`. A program takes and returns all parts, laid end to end along the dimension named above; each array names one. Nothing has to cross between parts.
Inputs may be any that keep to these rules, and one draw needn't show every extreme that they name: `target_slot_index`: A permutation: slots o * 8 to (o + 1) * 8 - 1 are those of owner o along blk. `active_block_table`: the first active_count[r] entries of row r are distinct target blocks, the rest are -1; in every row at most 8 live entries lie in slots of one owner, and some owner holds exactly 8 of them. `active_count`: some row block has 16 live entries.
All inputs are finite; a program needn't handle non-finite values.
Results may differ from a plain program's by a relative error of at most 0.0003.
Values may be sent and summed in bfloat16 or wider, within the bound.
A program may use at most 128 MiB of HBM per device.

v0:
```python
import functools
import math

import jax
import jax.numpy as jnp
from jax import lax
from jax.experimental import pallas as pl
from jax.experimental.pallas import tpu as pltpu
from jax.sharding import PartitionSpec as P

ITERS = 3
EPSILON = 0.01
FLOOR_VALUE = -1e30
TO_BITS = 1.0 / (EPSILON * math.log(2.0))
FROM_BITS = EPSILON * math.log(2.0)
MESH = pl.DeviceIdType.MESH
LIMIT = 48 * 1024 * 1024
VMEM = pltpu.VMEM


def vspec():
    return pl.BlockSpec(memory_space=pltpu.VMEM)


def sspec():
    return pl.BlockSpec(memory_space=pltpu.SMEM)


def log_join(peak, mass):
    safe = jnp.where(mass > 0.0, mass, 1.0)
    return jnp.where(mass > 0.0, peak + FROM_BITS * jnp.log2(safe), FLOOR_VALUE)


def log_sum(parts):
    peak = functools.reduce(jnp.maximum, parts)
    mass = functools.reduce(jnp.add, [jnp.exp2((p - peak) * TO_BITS) for p in parts])
    return peak + FROM_BITS * jnp.log2(mass)


def collapse(peak, mass):
    top = jnp.max(peak, axis=0, keepdims=True)
    total = jnp.sum(mass * jnp.exp2((peak - top) * TO_BITS), axis=0, keepdims=True)
    return log_join(top, total)


def gather_kernel(blocks, s_ref, all_ref, up_send, up_recv, down_send, down_recv, pair_send, pair_recv, own_sem):
    z = lax.axis_index("blk")
    c = lax.axis_index("pair")
    rows = s_ref.shape[0]
    half = rows // 2
    mine = pl.ds(pl.multiple_of(c * half, half), half)
    barrier = pltpu.get_barrier_semaphore()
    has_up = z + 1 < blocks
    has_down = z > 0

    @pl.when(has_up)
    def _():
        pl.semaphore_signal(barrier, inc=1, device_id={"blk": z + 1}, device_id_type=MESH)

    @pl.when(has_down)
    def _():
        pl.semaphore_signal(barrier, inc=1, device_id={"blk": z - 1}, device_id_type=MESH)

    pl.semaphore_signal(barrier, inc=1, device_id={"pair": 1 - c}, device_id_type=MESH)
    pl.semaphore_wait(barrier, 1 + has_up.astype(jnp.int32) + has_down.astype(jnp.int32))

    def hop(block, step, target, send, recv, first):
        return pltpu.make_async_remote_copy(
            src_ref=s_ref.at[mine] if first else all_ref.at[block, mine],
            dst_ref=all_ref.at[block, mine],
            send_sem=send.at[step],
            recv_sem=recv.at[step],
            device_id={"blk": target},
            device_id_type=MESH,
        )

    def across(block, slot):
        return pltpu.make_async_remote_copy(
            src_ref=all_ref.at[block, mine],
            dst_ref=all_ref.at[block, mine],
            send_sem=pair_send.at[slot],
            recv_sem=pair_recv.at[slot],
            device_id={"pair": 1 - c},
            device_id_type=MESH,
        )

    own = pltpu.make_async_copy(s_ref, all_ref.at[z], own_sem)
    own.start()

    @pl.when(has_up)
    def _():
        hop(z, 0, z + 1, up_send, up_recv, True).start()

    @pl.when(has_down)
    def _():
        hop(z, 0, z - 1, down_send, down_recv, True).start()

    for step in range(blocks - 1):
        below = z - 1 - step
        above = z + 1 + step

        @pl.when(below >= 0)
        def _():
            hop(below, step, z, up_send, up_recv, False).wait_recv()

            @pl.when(has_up)
            def _():
                hop(below, step + 1, z + 1, up_send, up_recv, False).start()

            across(below, below).start()

        @pl.when(above < blocks)
        def _():
            hop(above, step, z, down_send, down_recv, False).wait_recv()

            @pl.when(has_down)
            def _():
                hop(above, step + 1, z - 1, down_send, down_recv, False).start()

            across(above, above).start()

    own.wait()
    for block in range(blocks):

        @pl.when(block != z)
        def _():
            across(block, block).wait()

    for step in range(blocks):

        @pl.when(has_up & (z - step >= 0))
        def _():
            hop(z, step, z + 1, up_send, up_recv, True).wait_send()

        @pl.when(has_down & (z + step < blocks))
        def _():
            hop(z, step, z - 1, down_send, down_recv, True).wait_send()


def gather_rows(source, blocks):
    return pl.pallas_call(
        functools.partial(gather_kernel, blocks),
        out_shape=jax.ShapeDtypeStruct((blocks,) + source.shape, source.dtype),
        in_specs=[vspec()],
        out_specs=vspec(),
        scratch_shapes=[pltpu.SemaphoreType.DMA((blocks,)) for _ in range(6)]
        + [pltpu.SemaphoreType.DMA],
        compiler_params=pltpu.CompilerParams(
            collective_id=0, has_side_effects=True, vmem_limit_bytes=LIMIT
        ),
        name="gather_rows",
    )(source)


def tile_of(rows):
    return 256 if rows % 256 == 0 else rows


def absorb(scores, peak, mass, at):
    parts = scores.reshape(scores.shape[0] // 8, 8, scores.shape[1])
    old = peak[at]
    new = jnp.maximum(old, jnp.max(parts, axis=0))
    peak[at] = new
    mass[at] = mass[at] * jnp.exp2((old - new) * TO_BITS) + jnp.sum(
        jnp.exp2((parts - new[None]) * TO_BITS), axis=0
    )


def row_kernel(live, s_ref, t_ref, g_ref, out, peak, mass, spread):
    blocks, rows, depth = s_ref.shape
    slots, points, _ = t_ref.shape
    tile = tile_of(rows)
    peak[...] = jnp.full(peak.shape, FLOOR_VALUE, jnp.float32)
    mass[...] = jnp.zeros(mass.shape, jnp.float32)
    turned = jnp.transpose(g_ref[...])
    for q in range(slots):
        spread[q] = jnp.broadcast_to(turned[:, q : q + 1], (points, 128))

    @pl.loop(0, blocks * slots)
    def _(unit):
        r = unit // slots
        q = unit % slots

        @pl.when(live[unit] > 0)
        def _():
            bias = spread[q]
            bias = jnp.concatenate([bias] * (tile // 128), axis=1)
            for start in range(0, rows, tile):
                scores = lax.dot_general(
                    t_ref[q],
                    s_ref[r, start : start + tile],
                    (((1,), (1,)), ((), ())),
                    preferred_element_type=jnp.float32,
                )
                absorb(scores + bias, peak, mass, (r, slice(None), slice(start, start + tile)))

    for r in range(blocks):
        out[r : r + 1, :] = collapse(peak[r], mass[r])


def row_pass(live, rows_all, target, shifted):
    blocks, rows, _ = rows_all.shape
    slots, points, _ = target.shape
    return pl.pallas_call(
        row_kernel,
        out_shape=jax.ShapeDtypeStruct((blocks, rows), jnp.float32),
        in_specs=[sspec(), vspec(), vspec(), vspec()],
        out_specs=vspec(),
        scratch_shapes=[
            VMEM((blocks, 8, rows), jnp.float32),
            VMEM((blocks, 8, rows), jnp.float32),
            VMEM((slots, points, 128), jnp.float32),
        ],
        compiler_params=pltpu.CompilerParams(vmem_limit_bytes=LIMIT),
        name="row_pass",
    )(live, rows_all, target, shifted)


def column_kernel(live, s_ref, t_ref, r_ref, out, peak, mass, spread):
    blocks, rows, depth = s_ref.shape
    slots, points, _ = t_ref.shape
    tile = tile_of(rows)
    peak[...] = jnp.full(peak.shape, FLOOR_VALUE, jnp.float32)
    mass[...] = jnp.zeros(mass.shape, jnp.float32)
    turned = jnp.transpose(r_ref[...])
    for r in range(blocks):
        spread[r] = jnp.broadcast_to(turned[:, r : r + 1], (rows, 128))

    @pl.loop(0, blocks * slots)
    def _(unit):
        r = unit // slots
        q = unit % slots

        @pl.when(live[unit] > 0)
        def _():
            for start in range(0, rows, tile):
                bias = spread[r, start : start + tile]
                bias = jnp.concatenate([bias] * (points // 128), axis=1)
                scores = lax.dot_general(
                    s_ref[r, start : start + tile],
                    t_ref[q],
                    (((1,), (1,)), ((), ())),
                    preferred_element_type=jnp.float32,
                )
                absorb(scores - bias, peak, mass, (q,))

    for q in range(slots):
        out[q : q + 1, :] = collapse(peak[q], mass[q])


def column_pass(live, rows_all, target, row_log):
    blocks, rows, _ = rows_all.shape
    slots, points, _ = target.shape
    return pl.pallas_call(
        column_kernel,
        out_shape=jax.ShapeDtypeStruct((slots, points), jnp.float32),
        in_specs=[sspec(), vspec(), vspec(), vspec()],
        out_specs=vspec(),
        scratch_shapes=[
            VMEM((slots, 8, points), jnp.float32),
            VMEM((slots, 8, points), jnp.float32),
            VMEM((blocks, rows, 128), jnp.float32),
        ],
        compiler_params=pltpu.CompilerParams(vmem_limit_bytes=LIMIT),
        name="column_pass",
    )(live, rows_all, target, row_log)


def join_kernel(sizes, sign, x_ref, out, held, send, recv):
    names = list(sizes)
    total = math.prod(sizes.values())
    place = {n: lax.axis_index(n) for n in names}

    def peer(offset):
        ident = {}
        rest = offset
        for n in reversed(names):
            ident[n] = lax.rem(place[n] + rest % sizes[n], sizes[n])
            rest = rest // sizes[n]
        return ident

    barrier = pltpu.get_barrier_semaphore()
    for offset in range(1, total):
        pl.semaphore_signal(barrier, inc=1, device_id=peer(offset), device_id_type=MESH)
    pl.semaphore_wait(barrier, total - 1)
    copies = []
    for offset in range(1, total):
        copy = pltpu.make_async_remote_copy(
            src_ref=x_ref,
            dst_ref=held.at[offset - 1],
            send_sem=send.at[offset - 1],
            recv_sem=recv.at[offset - 1],
            device_id=peer(offset),
            device_id_type=MESH,
        )
        copy.start()
        copies.append(copy)
    for copy in copies:
        copy.wait()
    out[...] = sign * log_sum([x_ref[...]] + [held[i] for i in range(total - 1)])


def join_logs(x, sizes, ident, sign):
    total = math.prod(sizes.values())
    return pl.pallas_call(
        functools.partial(join_kernel, sizes, sign),
        out_shape=jax.ShapeDtypeStruct(x.shape, jnp.float32),
        in_specs=[vspec()],
        out_specs=vspec(),
        scratch_shapes=[
            VMEM((total - 1,) + x.shape, jnp.float32),
            pltpu.SemaphoreType.DMA((total - 1,)),
            pltpu.SemaphoreType.DMA((total - 1,)),
        ],
        compiler_params=pltpu.CompilerParams(
            collective_id=ident, has_side_effects=True, vmem_limit_bytes=LIMIT
        ),
        name="join_" + "_".join(sizes),
    )(x)


def fused_kernel(
    sizes, live, s_ref, t_ref, hs_ref, ht_ref, row_out, col_out,
    scores, rows_all, spread, row_mine, row_held, row_log, col_mine, col_held, columns,
    up_send, up_recv, down_send, down_recv, pair_send, pair_recv,
    row_send, row_recv, col_send, col_recv,
):
    blocks = sizes["blk"]
    z = lax.axis_index("blk")
    c = lax.axis_index("pair")
    rows = s_ref.shape[0]
    slots, points, _ = t_ref.shape
    half = rows // 2
    mine = pl.ds(pl.multiple_of(c * half, half), half)
    across_names = {"blk": blocks, "pair": sizes["pair"]}
    across_count = blocks * sizes["pair"]
    sub_count = sizes["sub"]

    def peer(offset):
        return {
            "blk": lax.rem(z + offset // sizes["pair"], blocks),
            "pair": lax.rem(c + offset % sizes["pair"], sizes["pair"]),
        }

    def side(offset):
        return {"sub": lax.rem(lax.axis_index("sub") + offset, sub_count)}

    barrier = pltpu.get_barrier_semaphore()
    for offset in range(1, across_count):
        pl.semaphore_signal(barrier, inc=1, device_id=peer(offset), device_id_type=MESH)
    for offset in range(1, sub_count):
        pl.semaphore_signal(barrier, inc=1, device_id=side(offset), device_id_type=MESH)
    pl.semaphore_wait(barrier, across_count + sub_count - 2)
    has_up = z + 1 < blocks
    has_down = z > 0

    def hop(block, step, target, send, recv, first):
        return pltpu.make_async_remote_copy(
            src_ref=s_ref.at[mine] if first else rows_all.at[block, mine],
            dst_ref=rows_all.at[block, mine],
            send_sem=send.at[step],
            recv_sem=recv.at[step],
            device_id={"blk": target},
            device_id_type=MESH,
        )

    def across(block):
        return pltpu.make_async_remote_copy(
            src_ref=rows_all.at[block, mine],
            dst_ref=rows_all.at[block, mine],
            send_sem=pair_send.at[block],
            recv_sem=pair_recv.at[block],
            device_id={"pair": 1 - c},
            device_id_type=MESH,
        )

    def fill(block, load):
        @pl.loop(0, slots)
        def _(q):
            shut = jnp.where(live[block * slots + q] > 0, 0.0, FLOOR_VALUE)
            for start in range(0, rows, 256):
                value = lax.dot_general(
                    t_ref[q],
                    load(start),
                    (((1,), (1,)), ((), ())),
                    preferred_element_type=jnp.float32,
                )
                scores[block, q, :, start : start + 256] = value * TO_BITS + shut

    @pl.when(has_up)
    def _():
        hop(z, 0, z + 1, up_send, up_recv, True).start()

    @pl.when(has_down)
    def _():
        hop(z, 0, z - 1, down_send, down_recv, True).start()

    turned = jnp.transpose(ht_ref[...]) * (-TO_BITS)
    for q in range(slots):
        spread[q] = jnp.broadcast_to(turned[:, q : q + 1], (points, 128))
    fill(z, lambda start: s_ref[start : start + 256])

    for step in range(blocks - 1):
        below = z - 1 - step
        above = z + 1 + step

        @pl.when(below >= 0)
        def _():
            hop(below, step, z, up_send, up_recv, False).wait_recv()

            @pl.when(has_up)
            def _():
                hop(below, step + 1, z + 1, up_send, up_recv, False).start()

            across(below).start()

        @pl.when(above < blocks)
        def _():
            hop(above, step, z, down_send, down_recv, False).wait_recv()

            @pl.when(has_down)
            def _():
                hop(above, step + 1, z - 1, down_send, down_recv, False).start()

            across(above).start()

        @pl.when(below >= 0)
        def _():
            across(below).wait_recv()
            fill(below, lambda start: rows_all[below, start : start + 256])

        @pl.when(above < blocks)
        def _():
            across(above).wait_recv()
            fill(above, lambda start: rows_all[above, start : start + 256])

    for iteration in range(ITERS):

        @pl.loop(0, blocks)
        def _(r):
            for start in range(0, rows, 256):
                span = slice(start, start + 256)
                peak = None
                for q in range(slots):
                    bias = jnp.concatenate([spread[q]] * 2, axis=1)
                    value = (scores[r, q, :, span] + bias).reshape(points // 8, 8, 256)
                    top = jnp.max(value, axis=0)
                    peak = top if peak is None else jnp.maximum(peak, top)
                mass = jnp.zeros((8, 256), jnp.float32)
                for q in range(slots):
                    bias = jnp.concatenate([spread[q]] * 2, axis=1)
                    value = (scores[r, q, :, span] + bias).reshape(points // 8, 8, 256)
                    mass = mass + jnp.sum(jnp.exp2(value - peak[None]), axis=0)
                top = jnp.max(peak, axis=0, keepdims=True)
                total = jnp.sum(mass * jnp.exp2(peak - top), axis=0, keepdims=True)
                row_mine[iteration, pl.ds(r, 1), span] = top + jnp.log2(total)

        copies = []
        for offset in range(1, across_count):
            copy = pltpu.make_async_remote_copy(
                src_ref=row_mine.at[iteration],
                dst_ref=row_held.at[iteration, offset - 1],
                send_sem=row_send.at[iteration, offset - 1],
                recv_sem=row_recv.at[iteration, offset - 1],
                device_id=peer(offset),
                device_id_type=MESH,
            )
            copy.start()
            copies.append(copy)
        for copy in copies:
            copy.wait()
        parts = [row_mine[iteration]] + [row_held[iteration, i] for i in range(across_count - 1)]
        row_log[...] = bit_sum(parts)

        for q in range(slots):

            @pl.loop(0, points // 64)
            def _(piece):
                part = pl.ds(pl.multiple_of(piece * 64, 64), 64)
                peak = jnp.full((64, 128), FLOOR_VALUE, jnp.float32)
                for r in range(blocks):
                    for start in range(0, rows, 128):
                        span = slice(start, start + 128)
                        peak = jnp.maximum(peak, scores[r, q, part, span] - row_log[r : r + 1, span])
                mass = jnp.zeros((64, 128), jnp.float32)
                for r in range(blocks):
                    for start in range(0, rows, 128):
                        span = slice(start, start + 128)
                        value = scores[r, q, part, span] - row_log[r : r + 1, span]
                        mass = mass + jnp.exp2(value - peak)
                top = jnp.max(peak, axis=1, keepdims=True)
                total = jnp.sum(mass * jnp.exp2(peak - top), axis=1, keepdims=True)
                columns[part, q : q + 1] = top + jnp.log2(total)

        col_mine[iteration] = jnp.transpose(columns[...])
        copies = []
        for offset in range(1, sub_count):
            copy = pltpu.make_async_remote_copy(
                src_ref=col_mine.at[iteration],
                dst_ref=col_held.at[iteration, offset - 1],
                send_sem=col_send.at[iteration, offset - 1],
                recv_sem=col_recv.at[iteration, offset - 1],
                device_id=side(offset),
                device_id_type=MESH,
            )
            copy.start()
            copies.append(copy)
        for copy in copies:
            copy.wait()
        total = bit_sum(
            [col_mine[iteration]] + [col_held[iteration, i] for i in range(sub_count - 1)]
        )
        named = total > 0.1 * FLOOR_VALUE
        shifted = jnp.where(named, -total, 0.0)
        if iteration < ITERS - 1:
            turned = jnp.transpose(shifted)
            for q in range(slots):
                spread[q] = jnp.broadcast_to(turned[:, q : q + 1], (points, 128))
        else:
            col_out[...] = jnp.where(named, ht_ref[...] + FROM_BITS * shifted, 0.0)

    row_out[...] = hs_ref[...] - FROM_BITS * row_log[pl.ds(z, 1), :]

    for block in range(blocks):

        @pl.when(block != z)
        def _():
            across(block).wait_send()

    for step in range(blocks):

        @pl.when(has_up & (z - step >= 0))
        def _():
            hop(z, step, z + 1, up_send, up_recv, True).wait_send()

        @pl.when(has_down & (z + step < blocks))
        def _():
            hop(z, step, z - 1, down_send, down_recv, True).wait_send()


def bit_sum(parts):
    peak = functools.reduce(jnp.maximum, parts)
    mass = functools.reduce(jnp.add, [jnp.exp2(p - peak) for p in parts])
    return peak + jnp.log2(mass)


def fused(live, source_rows, target, half_rows, half_cols, sizes):
    rows = source_rows.shape[0]
    slots, points, _ = target.shape
    blocks = sizes["blk"]
    peers = blocks * sizes["pair"] - 1
    sides = sizes["sub"] - 1
    dma = pltpu.SemaphoreType.DMA
    return pl.pallas_call(
        functools.partial(fused_kernel, sizes),
        out_shape=(
            jax.ShapeDtypeStruct((1, rows), jnp.float32),
            jax.ShapeDtypeStruct((slots, points), jnp.float32),
        ),
        in_specs=[sspec(), vspec(), vspec(), vspec(), vspec()],
        out_specs=(vspec(), vspec()),
        scratch_shapes=[
            VMEM((blocks, slots, points, rows), jnp.float32),
            VMEM((blocks,) + source_rows.shape, source_rows.dtype),
            VMEM((slots, points, 128), jnp.float32),
            VMEM((ITERS, blocks, rows), jnp.float32),
            VMEM((ITERS, peers, blocks, rows), jnp.float32),
            VMEM((blocks, rows), jnp.float32),
            VMEM((ITERS, slots, points), jnp.float32),
            VMEM((ITERS, sides, slots, points), jnp.float32),
            VMEM((points, slots), jnp.float32),
        ]
        + [dma((blocks,)) for _ in range(6)]
        + [dma((ITERS, peers)), dma((ITERS, peers)), dma((ITERS, sides)), dma((ITERS, sides))],
        compiler_params=pltpu.CompilerParams(
            collective_id=3, has_side_effects=True, vmem_limit_bytes=56 * 1024 * 1024
        ),
        name="fused_sinkhorn",
    )(live, source_rows, target, half_rows, half_cols)


def per_device(source, target, target_slot_index, active_block_table, active_count):
    blocks = lax.axis_size("blk")
    own_index = lax.axis_index("blk")
    source_rows = source[0]
    slots = target.shape[0]
    listlen = active_block_table.shape[1]
    names = jnp.arange(target_slot_index.shape[0], dtype=jnp.int32)
    table_matches = active_block_table[:, :, None] == names[None, None, :]
    slot_table = jnp.sum(jnp.where(table_matches, target_slot_index[None, None, :], 0), axis=2)
    live_mask = jnp.arange(listlen, dtype=jnp.int32)[None, :] < active_count[:, None]
    own_slots = own_index * slots + jnp.arange(slots, dtype=jnp.int32)
    live = jnp.any(
        live_mask[:, :, None] & (slot_table[:, :, None] == own_slots[None, None, :]), axis=1
    )
    named = jnp.any(live, axis=0)
    live_units = live.reshape(-1).astype(jnp.int32)
    half_rows = 0.5 * jnp.sum(jnp.square(source_rows.astype(jnp.float32)), axis=1)
    half_cols = 0.5 * jnp.sum(jnp.square(target.astype(jnp.float32)), axis=2)

    rows = source_rows.shape[0]
    sizes = {n: lax.axis_size(n) for n in ("blk", "sub", "pair")}
    held_bytes = 4 * blocks * rows * slots * target.shape[1]
    if held_bytes <= 32 * 1024 * 1024 and rows % 512 == 0 and sizes["pair"] == 2:
        return fused(live_units, source_rows, target, half_rows[None, :], half_cols, sizes)

    across = {"blk": blocks, "pair": lax.axis_size("pair")}
    along = {"sub": lax.axis_size("sub")}
    rows_all = gather_rows(source_rows, blocks)
    shifted = -half_cols
    for _ in range(ITERS):
        row_log = join_logs(row_pass(live_units, rows_all, target, shifted), across, 1, 1.0)
        shifted = join_logs(column_pass(live_units, rows_all, target, row_log), along, 2, -1.0)
    own_log = lax.dynamic_index_in_dim(row_log, own_index, 0, keepdims=False)
    row_pot = half_rows - own_log
    potential = jnp.where(named[:, None], half_cols + shifted, 0.0)
    return (row_pot[None, :], potential)


def solution(mesh):
    placed = (
        P(("groups", "blk"), "sub", None),
        P(("groups", "blk"), "pair", None),
        P("groups"),
        P("groups", None),
        P("groups"),
    )
    return jax.shard_map(
        per_device,
        mesh=mesh,
        in_specs=placed,
        out_specs=(P(("groups", "blk"), "sub"), P(("groups", "blk"), "pair")),
        check_vma=False,
    )
```

profile of v0, /device:TPU:0, one launch (start us, length us, event | category | flops | bytes accessed | tf_op | source)
XLA Modules:
  0.0 120.3 jit_solution(15446141689317210222)
XLA Ops:
  0.6 0.7 iota_compare_fusion.1
  1.4 0.9 select_reduce_fusion
  2.3 0.2 and_reduce_fusion
  2.5 0.6 reshape.44.live
  3.1 1.3 %multiply_reduce_fusion.1 = f32[1024]{0:T(1024)S(1)} fusion(bf16[1,1024,256]{2,1,0:T(8,128)(2,1)} %param.5), kind=kLoop, calls=%fused_computation.1 | loop fusion | flops 785408 | bytes 528384 | tf_op jit(solution)/shard_map/reduce_sum | solution.py:598
  4.4 0.6 broadcast_multiply_fusion.1
  5.0 1.6 %multiply_reduce_fusion = f32[8,256]{1,0:T(8,128)S(1)} fusion(bf16[8,256,256]{2,1,0:T(8,128)(2,1)} %t_ref.1), kind=kLoop, calls=%fused_computation | loop fusion | flops 1570816 | bytes 1056768 | tf_op jit(solution)/shard_map/reduce_sum | solution.py:599
  6.6 0.6 broadcast_multiply_fusion.ht_ref
  7.2 110.5 %fused_sinkhorn.1 = (f32[1,1024]{1,0:T(1,128)}, f32[8,256]{1,0:T(8,128)}) custom-call(s32[32]{0:T(128)} %reshape.44.live, bf16[1024,256]{1,0:T(8,128)(2,1)} %bitcast.3, bf16[8,256,256]{2,1,0:T(8,128)(2,1)} %t_ref.1, f32[1,1024]{1,0:T(1,128)} %bitcast.4, f32[8,256]{1,0:T(8,128)} %broadcast_multiply_fusion.ht_ref), custom_call_target="tpu_custom_call" | custom-call | tf_op jit(solution)/shard_map/fused_sinkhorn/pallas_call | solution.py:554
  117.7 1.3 %copy.9 = f32[1,1024]{1,0:T(1,128)} copy(f32[1,1024]{1,0:T(1,128)} %get-tuple-element.4) | data formatting | bytes 8192
  119.0 1.3 %copy.10 = f32[8,256]{1,0:T(8,128)} copy(f32[8,256]{1,0:T(8,128)} %get-tuple-element.5) | data formatting | bytes 16384
  (2 shorter events, 0.0 us)
where the time goes:
time: 121 us; the launch traced here: 120 us
  Pallas kernels  111 us (92%)
  other arithmetic  5.88 us (5%)
  local copies, waits for them, and re-layouts  3.19 us (3%)
    pallas_call x1, Pallas kernels, fused(): pl.pallas_call(functools.partial(fused_kernel, sizes), out_shape=(jax.Sha...  111 us
    unnamed x2, local copies, waits for them, and re-layouts  2.56 us

commit v1 on v0

--- a/solution.py
+++ b/solution.py
@@ -387,6 +387,23 @@
                 )
                 scores[block, q, :, start : start + 256] = value * TO_BITS + shut
 
+    def row_update(iteration, r):
+        for start in range(0, rows, 512):
+            span = slice(start, start + 512)
+            peak = jnp.full((8, 512), FLOOR_VALUE, jnp.float32)
+            mass = jnp.zeros((8, 512), jnp.float32)
+            for q in range(slots):
+                bias = jnp.concatenate([spread[q]] * 4, axis=1)
+                value = (scores[r, q, :, span] + bias).reshape(points // 8, 8, 512)
+                newer = jnp.maximum(peak, jnp.max(value, axis=0))
+                mass = mass * jnp.exp2(peak - newer) + jnp.sum(
+                    jnp.exp2(value - newer[None]), axis=0
+                )
+                peak = newer
+            top = jnp.max(peak, axis=0, keepdims=True)
+            total = jnp.sum(mass * jnp.exp2(peak - top), axis=0, keepdims=True)
+            row_mine[iteration, pl.ds(r, 1), span] = top + jnp.log2(total)
+
     @pl.when(has_up)
     def _():
         hop(z, 0, z + 1, up_send, up_recv, True).start()
@@ -398,9 +415,12 @@
     turned = jnp.transpose(ht_ref[...]) * (-TO_BITS)
     for q in range(slots):
         spread[q] = jnp.broadcast_to(turned[:, q : q + 1], (points, 128))
+    columns[...] = jnp.zeros(columns.shape, jnp.float32)
     fill(z, lambda start: s_ref[start : start + 256])
-
-    for step in range(blocks - 1):
+    row_update(0, z)
+
+    @pl.loop(0, blocks - 1)
+    def _(step):
         below = z - 1 - step
         above = z + 1 + step
 
@@ -424,37 +444,18 @@
 
             across(above).start()
 
-        @pl.when(below >= 0)
-        def _():
-            across(below).wait_recv()
-            fill(below, lambda start: rows_all[below, start : start + 256])
-
-        @pl.when(above < blocks)
-        def _():
-            across(above).wait_recv()
-            fill(above, lambda start: rows_all[above, start : start + 256])
-
-    for iteration in range(ITERS):
-
-        @pl.loop(0, blocks)
-        def _(r):
-            for start in range(0, rows, 256):
-                span = slice(start, start + 256)
-                peak = None
-                for q in range(slots):
-                    bias = jnp.concatenate([spread[q]] * 2, axis=1)
-                    value = (scores[r, q, :, span] + bias).reshape(points // 8, 8, 256)
-                    top = jnp.max(value, axis=0)
-                    peak = top if peak is None else jnp.maximum(peak, top)
-                mass = jnp.zeros((8, 256), jnp.float32)
-                for q in range(slots):
-                    bias = jnp.concatenate([spread[q]] * 2, axis=1)
-                    value = (scores[r, q, :, span] + bias).reshape(points // 8, 8, 256)
-                    mass = mass + jnp.sum(jnp.exp2(value - peak[None]), axis=0)
-                top = jnp.max(peak, axis=0, keepdims=True)
-                total = jnp.sum(mass * jnp.exp2(peak - top), axis=0, keepdims=True)
-                row_mine[iteration, pl.ds(r, 1), span] = top + jnp.log2(total)
-
+        for block, there in ((below, below >= 0), (above, above < blocks)):
+
+            @pl.when(there)
+            def _():
+                across(block).wait_recv()
+                fill(block, lambda start: rows_all[block, start : start + 256])
+                row_update(0, block)
+
+    lanes = lax.broadcasted_iota(jnp.int32, (points, 128), 1)
+
+    @pl.loop(0, ITERS)
+    def _(iteration):
         copies = []
         for offset in range(1, across_count):
             copy = pltpu.make_async_remote_copy(
@@ -472,27 +473,26 @@
         parts = [row_mine[iteration]] + [row_held[iteration, i] for i in range(across_count - 1)]
         row_log[...] = bit_sum(parts)
 
-        for q in range(slots):
-
-            @pl.loop(0, points // 64)
-            def _(piece):
-                part = pl.ds(pl.multiple_of(piece * 64, 64), 64)
-                peak = jnp.full((64, 128), FLOOR_VALUE, jnp.float32)
-                for r in range(blocks):
-                    for start in range(0, rows, 128):
-                        span = slice(start, start + 128)
-                        peak = jnp.maximum(peak, scores[r, q, part, span] - row_log[r : r + 1, span])
-                mass = jnp.zeros((64, 128), jnp.float32)
-                for r in range(blocks):
-                    for start in range(0, rows, 128):
-                        span = slice(start, start + 128)
-                        value = scores[r, q, part, span] - row_log[r : r + 1, span]
-                        mass = mass + jnp.exp2(value - peak)
-                top = jnp.max(peak, axis=1, keepdims=True)
-                total = jnp.sum(mass * jnp.exp2(peak - top), axis=1, keepdims=True)
-                columns[part, q : q + 1] = top + jnp.log2(total)
-
-        col_mine[iteration] = jnp.transpose(columns[...])
+        @pl.loop(0, slots)
+        def _(q):
+            peak = jnp.full((points, 128), FLOOR_VALUE, jnp.float32)
+            mass = jnp.zeros((points, 128), jnp.float32)
+            for r in range(blocks):
+                for base in range(0, rows, 1024):
+                    values = [
+                        scores[r, q, :, start : start + 128] - row_log[r : r + 1, start : start + 128]
+                        for start in range(base, min(base + 1024, rows), 128)
+                    ]
+                    newer = functools.reduce(jnp.maximum, values, peak)
+                    mass = mass * jnp.exp2(peak - newer)
+                    for value in values:
+                        mass = mass + jnp.exp2(value - newer)
+                    peak = newer
+            top = jnp.max(peak, axis=1, keepdims=True)
+            total = jnp.sum(mass * jnp.exp2(peak - top), axis=1, keepdims=True)
+            columns[...] = jnp.where(lanes == q, top + jnp.log2(total), columns[...])
+
+        col_mine[iteration] = jnp.transpose(columns[:, 0:slots])
         copies = []
         for offset in range(1, sub_count):
             copy = pltpu.make_async_remote_copy(
@@ -512,12 +512,17 @@
         )
         named = total > 0.1 * FLOOR_VALUE
         shifted = jnp.where(named, -total, 0.0)
-        if iteration < ITERS - 1:
+        col_out[...] = jnp.where(named, ht_ref[...] + FROM_BITS * shifted, 0.0)
+
+        @pl.when(iteration < ITERS - 1)
+        def _():
             turned = jnp.transpose(shifted)
             for q in range(slots):
                 spread[q] = jnp.broadcast_to(turned[:, q : q + 1], (points, 128))
-        else:
-            col_out[...] = jnp.where(named, ht_ref[...] + FROM_BITS * shifted, 0.0)
+
+            @pl.loop(0, blocks)
+            def _(r):
+                row_update(iteration + 1, r)
 
     row_out[...] = hs_ref[...] - FROM_BITS * row_log[pl.ds(z, 1), :]
 
@@ -568,7 +573,7 @@
             VMEM((blocks, rows), jnp.float32),
             VMEM((ITERS, slots, points), jnp.float32),
             VMEM((ITERS, sides, slots, points), jnp.float32),
-            VMEM((points, slots), jnp.float32),
+            VMEM((points, 128), jnp.float32),
         ]
         + [dma((blocks,)) for _ in range(6)]
         + [dma((ITERS, peers)), dma((ITERS, peers)), dma((ITERS, sides)), dma((ITERS, sides))],

time: 121 us -> 110 us (0.909)
  Pallas kernels: 111 us -> 99.9 us
    pallas_call x1, Pallas kernels: 111 us -> 99.9 us  [fused(): pl.pallas_call(functools.partial(fused_kernel, sizes), out_shape=(jax.Sha...]
where the time goes in v1:
time: 110 us
  Pallas kernels  99.9 us (91%)
  other arithmetic  5.88 us (5%)
  local copies, waits for them, and re-layouts  3.19 us (3%)
    pallas_call x1, Pallas kernels, fused(): pl.pallas_call(functools.partial(fused_kernel, sizes), out_shape=(jax.Sha...  99.9 us
    unnamed x2, local copies, waits for them, and re-layouts  2.56 us

profile of v1, /device:TPU:0, one launch (start us, length us, event | category | flops | bytes accessed | tf_op | source)
XLA Modules:
  0.0 109.7 jit_solution(17270333065004922385)
XLA Ops:
  0.6 0.7 iota_compare_fusion.1
  1.4 0.9 select_reduce_fusion
  2.3 0.2 and_reduce_fusion
  2.5 0.6 reshape.44.live
  3.1 1.3 %multiply_reduce_fusion.1 = f32[1024]{0:T(1024)S(1)} fusion(bf16[1,1024,256]{2,1,0:T(8,128)(2,1)} %param.5), kind=kLoop, calls=%fused_computation.1 | loop fusion | flops 785408 | bytes 528384 | tf_op jit(solution)/shard_map/reduce_sum | solution.py:603
  4.4 0.6 broadcast_multiply_fusion.1
  5.0 1.6 %multiply_reduce_fusion = f32[8,256]{1,0:T(8,128)S(1)} fusion(bf16[8,256,256]{2,1,0:T(8,128)(2,1)} %t_ref.1), kind=kLoop, calls=%fused_computation | loop fusion | flops 1570816 | bytes 1056768 | tf_op jit(solution)/shard_map/reduce_sum | solution.py:604
  6.6 0.6 broadcast_multiply_fusion.ht_ref
  7.2 99.9 %fused_sinkhorn.1 = (f32[1,1024]{1,0:T(1,128)}, f32[8,256]{1,0:T(8,128)}) custom-call(s32[32]{0:T(128)} %reshape.44.live, bf16[1024,256]{1,0:T(8,128)(2,1)} %bitcast.3, bf16[8,256,256]{2,1,0:T(8,128)(2,1)} %t_ref.1, f32[1,1024]{1,0:T(1,128)} %bitcast.4, f32[8,256]{1,0:T(8,128)} %broadcast_multiply_fusion.ht_ref), custom_call_target="tpu_custom_call" | custom-call | tf_op jit(solution)/shard_map/fused_sinkhorn/pallas_call | solution.py:559
  107.1 1.3 %copy.9 = f32[1,1024]{1,0:T(1,128)} copy(f32[1,1024]{1,0:T(1,128)} %get-tuple-element.4) | data formatting | bytes 8192
  108.4 1.3 %copy.10 = f32[8,256]{1,0:T(8,128)} copy(f32[8,256]{1,0:T(8,128)} %get-tuple-element.5) | data formatting | bytes 16384
  (2 shorter events, 0.0 us)
